TPU v7x, 512 devices: a whole 4x8x8 slice. The times are simulated.
512 devices in a mesh: elem: 64 (over z, x, core), spec: 8 (over y).
Axes of the slice: x: 4, y: 8, z: 8, core: 2. Of those that a mesh axis runs over, the one named last changes fastest.
Arguments:
- current: float32 [128, 64, 8192], P('spec', None, 'elem'), may hold values from -6 to 6
- previous: float32 [128, 64, 8192], P('spec', None, 'elem'), may hold values from -6 to 6
- velocity: float32 [3, 8192], P(None, 'elem'), may hold values from -4 to 4
- derivative: float32 [3, 64, 64], replicated, may hold values from -0.75 to 0.75
- lifting: float32 [64, 96], replicated, may hold values from -0.625 to 0.625
- stoichiometry: bfloat16 [128, 128], replicated, may hold values from -1 to 1
- send_tiles: int32 [64, 64, 2], P('elem'), may hold values from -1 to 31, as said below
- neighbours: int32 [6, 8192], P(None, 'elem'), may hold values from -1 to 639, as said below
- orientation: int32 [6, 8192], P(None, 'elem'), may hold values from 0 to 3
- refinement: int32 [8192], P('elem'), may hold values from 0 to 2
- tile_counts: int32 [2048], P('elem'), may hold values from 1 to 4
Outputs:
- next_state: float32 [128, 64, 8192], P('spec', None, 'elem')
Inputs may be any that keep to these rules, and one draw needn't show every extreme that they name: `send_tiles`: row p, column q: the first entries name tiles (0 to 31) of block p that block q reads, the rest are -1. Some block receives 2 tiles from every block. `neighbours`: -1 marks a boundary face. A value v below 128 names element v of the same block; a value of 128 or more names the element at that position of reach_b, which is always a listed tile slot (not -1).
All inputs are finite; a program needn't handle non-finite values.
Results may differ from a plain program's by a relative error of at most 0.0006.
Values may be sent and summed in bfloat16 or wider, within the bound.
A program may use at most 64 MiB of HBM per device.

v0:
```python
import jax
import jax.numpy as jnp
import numpy as np
from jax import lax
from jax.sharding import PartitionSpec as P

TILE = 4


TOP_PRECISION = lax.Precision.HIGHEST
DT_STEP = 0.2
SIGNS = np.array([-1.0, 1.0, -1.0, 1.0, -1.0, 1.0], np.float32)


def rotation_tables():
    tables = np.zeros((4, 16, 16), np.float32)
    for quarter in range(4):
        for across in range(4):
            for second in range(4):
                source = [
                    (across, second),
                    (second, 3 - across),
                    (3 - across, 3 - second),
                    (3 - second, across),
                ][quarter]
                tables[quarter, across + 4 * second, source[0] + 4 * source[1]] = 1.0
    return tables


def face_node(face_index, first, second):
    fixed_value = 0 if face_index % 2 == 0 else 3
    if face_index < 2:
        return fixed_value + 4 * first + 16 * second
    if face_index < 4:
        return first + 4 * fixed_value + 16 * second
    return first + 4 * second + 16 * fixed_value


def trace_table(flipped):
    table = np.zeros((96, 64), np.float32)
    for face_index in range(6):
        source_face = face_index ^ 1 if flipped else face_index
        for first in range(4):
            for second in range(4):
                table[
                    16 * face_index + first + 4 * second, face_node(source_face, first, second)
                ] = 1.0
    return table


def transport(masked, incoming, velocity, derivative, lifting, neighbours, orientation, refinement):
    owned_count = neighbours.shape[1]
    chemical_species = masked.shape[0]
    node_count = masked.shape[1]
    stacked_ops = derivative.reshape(3 * node_count, node_count)
    slopes = jnp.einsum("qb,tbz->tqz", stacked_ops, masked, precision=TOP_PRECISION).reshape(
        chemical_species, 3, node_count, owned_count
    )
    volume = -jnp.sum(velocity[None, :, None, :] * slopes, axis=1)
    own_table = jnp.asarray(trace_table(False))
    far_table = jnp.asarray(trace_table(True))
    inner_trace = jnp.einsum("ub,tbz->tuz", own_table, masked, precision=TOP_PRECISION).reshape(
        chemical_species, 6, 16, owned_count
    )
    local_far = jnp.einsum("ub,tbz->tuz", far_table, masked, precision=TOP_PRECISION)
    remote_far = jnp.einsum("ub,tbz->tuz", far_table, incoming, precision=TOP_PRECISION)
    far_traces = jnp.concatenate([local_far, remote_far], axis=2).reshape(
        chemical_species, 6, 16, -1
    )
    reach_count = far_traces.shape[3]
    outer_list = []
    for face_index in range(6):
        partner = jnp.clip(neighbours[face_index], 0, reach_count - 1)
        picked = jnp.take(far_traces[:, face_index], partner, axis=2)
        outer_list.append(jnp.where(neighbours[face_index][None, None, :] >= 0, picked, 0.0))
    outer_trace = jnp.stack(outer_list, axis=1)
    rotations = rotation_tables()
    turned = jnp.zeros(outer_trace.shape, jnp.float32)
    for quarter in range(4):
        rotated = jnp.einsum(
            "xy,sfye->sfxe", jnp.asarray(rotations[quarter]), outer_trace, precision=TOP_PRECISION
        )
        turned = turned + jnp.where((orientation == quarter)[None, :, None, :], rotated, 0.0)
    normal = jnp.asarray(SIGNS)[:, None] * jnp.repeat(velocity, 2, axis=0)
    inflow = jnp.minimum(normal, 0.0)
    jump_contribution = inflow[None, :, None, :] * (inner_trace - turned)
    face_contribution = jnp.einsum(
        "hu,muw->mhw",
        lifting,
        jump_contribution.reshape(chemical_species, 96, owned_count),
        precision=TOP_PRECISION,
    )
    metric = jnp.where(refinement == 0, 1.0, jnp.where(refinement == 1, 2.0, 4.0))
    return metric[None, None, :] * (volume + face_contribution)


def per_device(
    current,
    previous,
    velocity,
    derivative,
    lifting,
    stoichiometry,
    send_tiles,
    neighbours,
    orientation,
    refinement,
    tile_counts,
):
    local_species, node_count, owned_count = current.shape
    tile_total = tile_counts.shape[0]
    alive = (
        jnp.arange(owned_count, dtype=jnp.int32) % TILE < jnp.repeat(tile_counts, TILE)
    ).astype(jnp.float32)[None, None, :]
    masked = current * alive
    chosen = jnp.clip(send_tiles[0], 0, tile_total - 1).reshape(-1)
    tiled_state = masked.reshape(local_species, node_count, tile_total, TILE)
    outgoing = jnp.take(tiled_state, chosen, axis=2).reshape(local_species, node_count, -1)
    incoming = lax.all_to_all(
        outgoing.astype(jnp.bfloat16), "elem", split_axis=2, concat_axis=2, tiled=True
    ).astype(outgoing.dtype)
    saturated = (masked / (1.0 + jnp.abs(masked))).astype(jnp.bfloat16)
    flat_states = saturated.reshape(local_species, node_count * owned_count)
    own_columns = lax.dynamic_slice_in_dim(
        stoichiometry, lax.axis_index("spec") * local_species, local_species, 1
    )
    reaction = jnp.dot(
        own_columns.T,
        lax.all_gather(flat_states, "spec", axis=0, tiled=True),
        preferred_element_type=jnp.float32,
    ).reshape(local_species, node_count, owned_count)
    moved = transport(
        masked, incoming, velocity, derivative, lifting, neighbours, orientation, refinement
    )
    rates = (moved + reaction) * alive
    return alive * (0.75 * previous + 0.25 * (masked + DT_STEP * rates))


def solution(mesh):
    placed = (
        P("spec", None, "elem"),
        P("spec", None, "elem"),
        P(None, "elem"),
        P(),
        P(),
        P(),
        P("elem", None, None),
        P(None, "elem"),
        P(None, "elem"),
        P("elem"),
        P("elem"),
    )
    return jax.shard_map(
        per_device, mesh=mesh, in_specs=placed, out_specs=P("spec", None, "elem"), check_vma=False
    )
```

profile of v0, /device:TPU:1, one launch (start us, length us, event | category | flops | bytes accessed | tf_op | source)
XLA Modules:
  0.0 138.1 jit_solution(15373013863094414885)
XLA Ops:
  6.5 0.7 broadcast_clamp_fusion
  7.3 0.1 copy.50
  7.4 0.1 min.70
  7.5 0.1 min.68
  7.6 0.7 broadcast_in_dim.122
  8.4 0.1 reshape.181
  8.5 1.2 divide_convert_fusion
  9.7 0.5 copy.51
  10.2 0.1 broadcast_in_dim.129
  10.3 0.1 broadcast_in_dim.130
  10.4 1.0 gather_fusion
  11.4 2.8 %fusion = bf16[16,64,512]{1,0,2:T(8,128)(2,1)} fusion(bf16[128,16,64,4]{2,1,3,0:T(8,128)(2,1)S(1)} %gather_fusion, pred[512]{0:T(512)(128)(4,1)S(1)} %broadcast_in_dim.130), kind=kLoop, calls=%fused_computation.8 | loop fusion | flops 524288 | bytes 2097664 | tf_op jit(solution)/shard_map/convert_element_type | solution.py:120
  14.2 4.7 %reshape.273 = bf16[64,2,4096]{2,1,0:T(2,128)(2,1)} reshape(bf16[512,16,64]{2,1,0:T(8,128)(2,1)} %bitcast.178) | data formatting | bytes 2097152
  18.8 15.2 %all-to-all-start = ((bf16[64,2,4096]{2,1,0:T(2,128)(2,1)}), bf16[64,2,4096]{2,1,0:T(2,128)(2,1)}, u32[]{:S(2)}, u32[]{:S(2)}) async-start(bf16[64,2,4096]{2,1,0:T(2,128)(2,1)} %reshape.273), calls=%async_computation | async-start | bytes 2097152 | tf_op jit(solution)/shard_map/all_to_all | solution.py:119
  34.0 0.0 all-gather.2.cloned.1.call-start
  34.1 0.0 copy-start.10
  34.1 0.9 copy.90
  35.0 0.0 all-gather.2.cloned.1.call-update
  35.0 0.6 compare_and_fusion
  35.6 0.6 pad_clamp_fusion.4
  36.2 0.0 copy-start.28
  36.2 1.4 %fusion.26 = f32[16,128,192]{1,2,0:T(8,128)S(1)} fusion(f32[16,64,128]{2,1,0:T(8,128)S(1)} %get-tuple-element.19, f32[192,64,1]{1,0,2:T(8,128)S(1)} %bitcast.175), kind=kOutput, calls=%fused_computation.94 | convolution fusion | flops 301989888 | bytes 2146304 | tf_op jit(solution)/shard_map/qb,tbz->tqz/dot_general | solution.py:56
  37.6 1.0 multiply_reduce_fusion
  38.6 0.5 compare_select_fusion.9
  39.1 0.5 broadcast_compare_fusion.3
  39.6 1.7 %convolution_bitcast_fusion = f32[16,96,128]{2,1,0:T(8,128)} fusion(f32[16,64,128]{2,1,0:T(8,128)S(1)} %get-tuple-element.19, f32[96,64,1]{0,1,2:T(8,128)S(1)} %copy-done.7), kind=kOutput, calls=%fused_computation.24 | convolution fusion | flops 150994944 | bytes 1335296 | tf_op jit(solution)/shard_map/ub,tbz->tuz/dot_general | solution.py:65
  41.3 0.8 fusion.27
  42.2 0.1 multiply_minimum_fusion
  42.3 19.6 %all-to-all-done = bf16[64,2,4096]{2,1,0:T(2,128)(2,1)} async-done(((bf16[64,2,4096]{2,1,0:T(2,128)(2,1)}), bf16[64,2,4096]{2,1,0:T(2,128)(2,1)}, u32[]{:S(2)}, u32[]{:S(2)}) %all-to-all-start) | async-done | bytes 1048608 | tf_op jit(solution)/shard_map/all_to_all | solution.py:119
  61.9 3.8 %reshape.274 = bf16[512,16,64]{2,1,0:T(8,128)(2,1)S(1)} reshape(bf16[64,2,4096]{2,1,0:T(2,128)(2,1)} %all-to-all-done) | data formatting | bytes 2097152
  65.7 2.3 %fusion.3 = f32[16,96,512]{2,1,0:T(8,128)S(1)} fusion(f32[96,64,1]{0,1,2:T(8,128)S(1)} %copy-done.7, bf16[16,64,512]{1,0,2:T(8,128)(2,1)S(1)} %bitcast.179), kind=kOutput, calls=%fused_computation.12 | convolution fusion | flops 603979776 | bytes 4218880 | tf_op jit(solution)/shard_map/ub,tbz->tuz/dot_general | solution.py:66
  68.1 0.4 pad_maximum_fusion
  68.5 1.5 %fusion.25 = (f32[16,1,16,640]{3,2,1,0:T(8,128)S(1)}, f32[16,1,16,640]{3,2,1,0:T(8,128)S(1)}, f32[16,1,16,640]{3,2,1,0:T(8,128)S(1)}, f32[16,1,16,640]{3,2,1,0:T...) fusion(f32[16,6,16,640]{3,2,1,0:T(8,128)S(1)} %bitcast.177), kind=kLoop, calls=%fused_computation.93 | loop fusion | bytes 7864320 | tf_op jit(solution)/shard_map/slice | solution.py:74
  70.0 4.1 %copy.77 = f32[16,1,16,640]{2,0,3,1:T(8,128)} copy(f32[16,1,16,640]{3,2,1,0:T(8,128)} %get-tuple-element.25) | data formatting | bytes 1310720
  74.1 4.3 %gather_fusion.1 = f32[128,16,16]{2,1,0:T(8,128)} fusion(f32[16,16,640]{1,0,2:T(8,128)} %bitcast.184, s32[1024]{0:T(1024)} %get-tuple-element.51), kind=kCustom, calls=%fused_computation.clone | custom fusion | bytes 262656 | tf_op jit(solution)/shard_map/jit(_take)/gather | solution.py:74
  78.4 1.6 %copy.55 = f32[128,16,16]{0,2,1:T(8,128)S(1)} copy(f32[128,16,16]{2,1,0:T(8,128)} %gather_fusion.1) | data formatting | bytes 262144 | tf_op jit(solution)/shard_map/jit(_take)/gather | solution.py:74
  80.0 4.1 %copy.78 = f32[16,1,16,640]{2,0,3,1:T(8,128)} copy(f32[16,1,16,640]{3,2,1,0:T(8,128)} %get-tuple-element.24) | data formatting | bytes 1310720
  84.1 4.2 %gather_fusion.2 = f32[128,16,16]{2,1,0:T(8,128)} fusion(f32[16,16,640]{1,0,2:T(8,128)} %bitcast.181, s32[1024]{0:T(1024)S(1)} %get-tuple-element.50), kind=kCustom, calls=%fused_computation.1.clone | custom fusion | bytes 262656 | tf_op jit(solution)/shard_map/jit(_take)/gather | solution.py:74
  88.3 2.3 %copy.57 = f32[128,16,16]{0,2,1:T(8,128)} copy(f32[128,16,16]{2,1,0:T(8,128)} %gather_fusion.2) | data formatting | bytes 262144 | tf_op jit(solution)/shard_map/jit(_take)/gather | solution.py:74
  90.5 4.1 %copy.79 = f32[16,1,16,640]{2,0,3,1:T(8,128)} copy(f32[16,1,16,640]{3,2,1,0:T(8,128)} %get-tuple-element.23) | data formatting | bytes 1310720
  94.6 4.2 %gather_fusion.3 = f32[128,16,16]{2,1,0:T(8,128)} fusion(f32[16,16,640]{1,0,2:T(8,128)} %bitcast.185, s32[1024]{0:T(1024)S(1)} %get-tuple-element.49), kind=kCustom, calls=%fused_computation.2.clone | custom fusion | bytes 262656 | tf_op jit(solution)/shard_map/jit(_take)/gather | solution.py:74
  98.8 2.3 %copy.59 = f32[128,16,16]{0,2,1:T(8,128)} copy(f32[128,16,16]{2,1,0:T(8,128)} %gather_fusion.3) | data formatting | bytes 262144 | tf_op jit(solution)/shard_map/jit(_take)/gather | solution.py:74
  101.1 3.2 %copy.80 = f32[16,1,16,640]{2,0,3,1:T(8,128)} copy(f32[16,1,16,640]{3,2,1,0:T(8,128)S(1)} %get-tuple-element.22) | data formatting | bytes 1310720
  104.2 4.2 %gather_fusion.4 = f32[128,16,16]{2,1,0:T(8,128)} fusion(f32[16,16,640]{1,0,2:T(8,128)} %bitcast.182, s32[1024]{0:T(1024)S(1)} %get-tuple-element.48), kind=kCustom, calls=%fused_computation.3.clone | custom fusion | bytes 262656 | tf_op jit(solution)/shard_map/jit(_take)/gather | solution.py:74
  108.4 1.6 %copy.61 = f32[128,16,16]{0,2,1:T(8,128)S(1)} copy(f32[128,16,16]{2,1,0:T(8,128)} %gather_fusion.4) | data formatting | bytes 262144 | tf_op jit(solution)/shard_map/jit(_take)/gather | solution.py:74
  110.0 3.2 %copy.81 = f32[16,1,16,640]{2,0,3,1:T(8,128)} copy(f32[16,1,16,640]{3,2,1,0:T(8,128)S(1)} %get-tuple-element.21) | data formatting | bytes 1310720
  113.2 3.1 %gather_fusion.5 = f32[128,16,16]{2,1,0:T(8,128)S(1)} fusion(f32[16,16,640]{1,0,2:T(8,128)} %bitcast.186, s32[1024]{0:T(1024)S(1)} %get-tuple-element.47), kind=kCustom, calls=%fused_computation.4.clone | custom fusion | bytes 262656 | tf_op jit(solution)/shard_map/jit(_take)/gather | solution.py:74
  116.3 0.4 copy.63
  116.8 0.0 copy-start.15
  116.8 3.2 %copy.82 = f32[16,1,16,640]{2,0,3,1:T(8,128)} copy(f32[16,1,16,640]{3,2,1,0:T(8,128)S(1)} %get-tuple-element.20) | data formatting | bytes 1310720
  120.0 3.2 %gather_fusion.6 = f32[128,16,16]{2,1,0:T(8,128)S(1)} fusion(f32[16,16,640]{1,0,2:T(8,128)} %bitcast.183, s32[1024]{0:T(1024)S(1)} %get-tuple-element.46), kind=kCustom, calls=%fused_computation.5.clone | custom fusion | bytes 262656 | tf_op jit(solution)/shard_map/jit(_take)/gather | solution.py:74
  123.2 0.4 copy.65
  123.8 0.8 convolution_select_fusion
  124.6 0.8 convolution_select_fusion.1
  125.4 0.0 copy-start.8
  125.4 0.8 convolution_select_fusion.2
  126.3 0.0 copy-start.3
  126.3 0.0 copy-start.1
  126.3 0.9 fusion.11
  127.2 0.0 copy-start.4
  127.2 0.0 all-gather.2.cloned.1.call-done
  127.3 2.1 %convolution_bitcast_fusion.1 = f32[2,8,64,128]{3,1,2,0:T(8,128)S(1)} fusion(bf16[128,8192]{1,0:T(8,128)(2,1)} %all-gather.2.cloned.1.call-done, bf16[128,128]{1,0:T(8,128)(2,1)S(1)} %copy-done.8, s32[]{:T(128)S(6)} %select_n.101), kind=kOutput, calls=%fused_computation.25 | convolution fusion | flops 33554432 | bytes 2654212 | tf_op jit(solution)/shard_map/dot_general | solution.py:127
  129.4 0.1 copy.84
  129.6 1.6 %fusion.20 = f32[16,64,128]{2,1,0:T(8,128)} fusion(f32[16,64,128]{2,1,0:T(8,128)S(1)} %get-tuple-element.19, f32[16,64,128]{2,1,0:T(8,128)S(1)} %bitcast.189, f32[16,96,128]{2,1,0:T(8,128)S(1)} %bitcast.188, f32[16,64,128]{2,1,0:T(8,128)S(1)} %copy-done.3, f32[16,64,128]{2,1,0:T(8,128)S(1)} %copy-done.4, f32[128]{0:T(128)S(1)} %copy-done.27, ...), kind=kOutput, calls=%fused_computation.35 | convolution fusion | flops 152436736 | bytes 3433472 | tf_op jit(solution)/shard_map/hu,muw->mhw/dot_general | solution.py:87
  (68 shorter events, 0.3 us)
Async XLA Ops:
  6.5 29.7 %copy-start = (f32[3,64,64]{2,1,0:T(8,128)S(1)}, f32[3,64,64]{2,1,0:T(8,128)}, u32[]{:S(2)}) copy-start(f32[3,64,64]{2,1,0:T(8,128)} %param.23) | copy-start | bytes 147460
  8.5 1.2 copy-start.19
  14.2 20.8 %copy-start.11 = (s32[6,128]{1,0:T(8,128)S(1)}, s32[6,128]{1,0:T(8,128)}, u32[]{:S(2)}) copy-start(s32[6,128]{1,0:T(8,128)} %param.27) | copy-start | bytes 9220
  18.8 18.8 %copy-start.16 = (f32[3,128]{1,0:T(4,128)S(1)}, f32[3,128]{1,0:T(4,128)}, u32[]{:S(2)}) copy-start(f32[3,128]{1,0:T(4,128)} %param.22) | copy-start | bytes 4612
  18.8 19.8 %copy-start.29 = (s32[128]{0:T(128)S(1)}, s32[128]{0:T(128)}, u32[]{:S(2)}) copy-start(s32[128]{0:T(128)} %param.29) | copy-start | bytes 1540
  18.8 20.3 %copy-start.18 = (s32[6,128]{1,0:T(8,128)S(1)}, s32[6,128]{1,0:T(8,128)}, u32[]{:S(2)}) copy-start(s32[6,128]{1,0:T(8,128)} %param.28) | copy-start | bytes 9220
  18.8 20.8 %copy-start.7 = (f32[96,64,1]{0,1,2:T(8,128)S(1)}, f32[96,64,1]{0,1,2:T(8,128)}, u32[]{:S(2)}) copy-start(f32[96,64,1]{0,1,2:T(8,128)} %constant.102) | copy-start | bytes 73732
  18.8 43.1 %all-to-all-start = ((bf16[64,2,4096]{2,1,0:T(2,128)(2,1)}), bf16[64,2,4096]{2,1,0:T(2,128)(2,1)}, u32[]{:S(2)}, u32[]{:S(2)}) async-start(bf16[64,2,4096]{2,1,0:T(2,128)(2,1)} %reshape.273), calls=%async_computation | async-start | bytes 2097152 | tf_op jit(solution)/shard_map/all_to_all | solution.py:119
  34.0 93.2 %all-gather.2.cloned.1.call-start = ((), (), s32[]{:S(2)}) async-start(), calls=%async_computation.1 | async-start | bytes 2359296 | tf_op jit(solution)/shard_map/all_gather | solution.py:129
  34.1 7.3 %copy-start.10 = (f32[96,64,1]{0,1,2:T(8,128)S(1)}, f32[96,64,1]{0,1,2:T(8,128)}, u32[]{:S(2)}) copy-start(f32[96,64,1]{0,1,2:T(8,128)} %constant.101) | copy-start | bytes 73732
  36.2 6.0 %copy-start.28 = (f32[6]{0:T(128)S(1)}, f32[6]{0:T(128)}, u32[]{:S(2)}) copy-start(f32[6]{0:T(128)} %constant.98.clone) | copy-start | bytes 76
  65.7 2.3 %copy-start.2 = (f32[16,96,128]{2,1,0:T(8,128)S(1)}, f32[16,96,128]{2,1,0:T(8,128)}, u32[]{:S(2)}) copy-start(f32[16,96,128]{2,1,0:T(8,128)} %convolution_bitcast_fusion) | copy-start | bytes 2359300
  116.8 6.8 %copy-start.26 = (pred[128]{0:T(512)(128)(4,1)S(1)}, pred[128]{0:T(512)(128)(4,1)}, u32[]{:S(2)}) copy-start(pred[128]{0:T(512)(128)(4,1)} %get-tuple-element.36) | copy-start | bytes 388
  116.8 6.9 %copy-start.5 = (f32[128,16,16]{0,2,1:T(8,128)S(1)}, f32[128,16,16]{0,2,1:T(8,128)}, u32[]{:S(2)}) copy-start(f32[128,16,16]{0,2,1:T(8,128)} %copy.57) | copy-start | bytes 393220
  116.8 6.9 %copy-start.25 = (pred[128]{0:T(512)(128)(4,1)S(1)}, pred[128]{0:T(512)(128)(4,1)}, u32[]{:S(2)}) copy-start(pred[128]{0:T(512)(128)(4,1)} %get-tuple-element.38) | copy-start | bytes 388
  116.8 6.9 %copy-start.6 = (f32[128,16,16]{0,2,1:T(8,128)S(1)}, f32[128,16,16]{0,2,1:T(8,128)}, u32[]{:S(2)}) copy-start(f32[128,16,16]{0,2,1:T(8,128)} %copy.59) | copy-start | bytes 393220
  116.8 6.9 %copy-start.24 = (pred[128]{0:T(512)(128)(4,1)S(1)}, pred[128]{0:T(512)(128)(4,1)}, u32[]{:S(2)}) copy-start(pred[128]{0:T(512)(128)(4,1)} %get-tuple-element.40) | copy-start | bytes 388
  116.8 6.9 %copy-start.23 = (pred[128]{0:T(512)(128)(4,1)S(1)}, pred[128]{0:T(512)(128)(4,1)}, u32[]{:S(2)}) copy-start(pred[128]{0:T(512)(128)(4,1)} %get-tuple-element.42) | copy-start | bytes 388
  116.8 6.9 %copy-start.22 = (pred[128]{0:T(512)(128)(4,1)S(1)}, pred[128]{0:T(512)(128)(4,1)}, u32[]{:S(2)}) copy-start(pred[128]{0:T(512)(128)(4,1)} %get-tuple-element.44) | copy-start | bytes 388
  116.8 7.0 %copy-start.21 = (pred[128]{0:T(512)(128)(4,1)S(1)}, pred[128]{0:T(512)(128)(4,1)}, u32[]{:S(2)}) copy-start(pred[128]{0:T(512)(128)(4,1)} %get-tuple-element.6) | copy-start | bytes 388
  116.8 7.0 %copy-start.15 = (f32[16,16,1,1]{1,0,3,2:T(8,128)S(1)}, f32[16,16,1,1]{1,0,3,2:T(8,128)}, u32[]{:S(2)}) copy-start(f32[16,16,1,1]{1,0,3,2:T(8,128)} %constant.106) | copy-start | bytes 3076
  120.0 4.6 %copy-start.14 = (f32[16,16,1,1]{1,0,3,2:T(8,128)S(1)}, f32[16,16,1,1]{1,0,3,2:T(8,128)}, u32[]{:S(2)}) copy-start(f32[16,16,1,1]{1,0,3,2:T(8,128)} %constant.105) | copy-start | bytes 3076
  120.0 5.4 %copy-start.13 = (f32[16,16,1,1]{1,0,3,2:T(8,128)S(1)}, f32[16,16,1,1]{1,0,3,2:T(8,128)}, u32[]{:S(2)}) copy-start(f32[16,16,1,1]{1,0,3,2:T(8,128)} %constant.104) | copy-start | bytes 3076
  123.6 2.7 %copy-start.12 = (f32[16,16,1,1]{1,0,3,2:T(8,128)S(1)}, f32[16,16,1,1]{1,0,3,2:T(8,128)}, u32[]{:S(2)}) copy-start(f32[16,16,1,1]{1,0,3,2:T(8,128)} %constant.103) | copy-start | bytes 3076
  123.6 2.7 %copy-start.17 = (pred[6,128]{1,0:T(8,128)(4,1)S(1)}, pred[6,128]{1,0:T(8,128)(4,1)}, u32[]{:S(2)}) copy-start(pred[6,128]{1,0:T(8,128)(4,1)} %get-tuple-element.26) | copy-start | bytes 2308
  125.4 1.9 %copy-start.8 = (bf16[128,128]{1,0:T(8,128)(2,1)S(1)}, bf16[128,128]{1,0:T(8,128)(2,1)}, u32[]{:S(2)}) copy-start(bf16[128,128]{1,0:T(8,128)(2,1)} %param.25) | copy-start | bytes 98308
  126.3 3.3 %copy-start.3 = (f32[16,64,128]{2,1,0:T(8,128)S(1)}, f32[16,64,128]{2,1,0:T(8,128)}, u32[]{:S(2)}) copy-start(f32[16,64,128]{2,1,0:T(8,128)} %multiply_reduce_fusion) | copy-start | bytes 1572868
  126.3 3.3 %copy-start.20 = (f32[128]{0:T(128)S(1)}, f32[128]{0:T(128)}, u32[]{:S(2)}) copy-start(f32[128]{0:T(128)} %copy-done.19) | copy-start | bytes 1540
  126.3 3.3 %copy-start.27 = (f32[128]{0:T(128)S(1)}, f32[128]{0:T(128)}, u32[]{:S(2)}) copy-start(f32[128]{0:T(128)} %compare_select_fusion.9) | copy-start | bytes 1540
  126.3 4.9 %copy-start.1 = (f32[3,64,64]{2,1,0:T(8,128)S(1)}, f32[3,64,64]{2,1,0:T(8,128)}, u32[]{:S(2)}) copy-start(f32[3,64,64]{2,1,0:T(8,128)} %param.23) | copy-start | bytes 147460
  127.2 2.3 %copy-start.4 = (f32[16,64,128]{2,1,0:T(8,128)S(1)}, f32[16,64,128]{2,1,0:T(8,128)}, u32[]{:S(2)}) copy-start(f32[16,64,128]{2,1,0:T(8,128)} %param.21) | copy-start | bytes 1572868
  127.2 2.3 %copy-start.9 = (f32[64,96]{1,0:T(8,128)S(1)}, f32[64,96]{1,0:T(8,128)}, u32[]{:S(2)}) copy-start(f32[64,96]{1,0:T(8,128)} %param.24) | copy-start | bytes 73732
Sparse Core Ops, SparseCore 0:
  36.9 40.8 all-gather.1
where the time goes:
time: 139 us; the launch traced here: 138 us
  local copies, waits for them, and re-layouts  67.4 us (48%)
  waiting for transfers between devices  19.6 us (14%)
  starting transfers between devices  15.2 us (11%)
  between operations  14 us (10%)
  matrix products  13.3 us (10%)
  other arithmetic  8.46 us (6%)
    gather x12, local copies, waits for them, and re-layouts, transport(): picked = jnp.take(far_traces[:, face_index], partner, axis=2)  31.8 us
    unnamed x70, local copies, waits for them, and re-layouts  31.3 us
    all_to_all x1, waiting for transfers between devices, per_device(): lax.all_to_all(outgoing.astype(jnp.bfloat16), 'elem', split_axis=2, conca...  19.6 us
    all_to_all x1, starting transfers between devices, per_device(): lax.all_to_all(outgoing.astype(jnp.bfloat16), 'elem', split_axis=2, conca...  15.2 us
    dot_general x4, matrix products, transport(): jnp.einsum('xy,sfye->sfxe', jnp.asarray(rotations[quarter]), outer_trace,...  3.29 us
    convert_element_type x1, other arithmetic, per_device(): outgoing.astype(jnp.bfloat16)  2.79 us
  transfers between devices with their start and end apart: 2, of which 1 were waited for; matrix products, arithmetic and copies ran while one was open for 53% of the time, Pallas kernels for 0%

commit v1 on v0

v1 whole, which is shorter than its diff:
```python
import functools

import jax
import jax.numpy as jnp
import numpy as np
from jax import lax
from jax.experimental import pallas as pl
from jax.experimental.pallas import tpu as pltpu
from jax.sharding import PartitionSpec as P

MESH = pl.DeviceIdType.MESH
F32 = jnp.float32
BF16 = jnp.bfloat16

NZ, NX, NY = 8, 4, 8
SPEC = 16
NODES = 64
ELEM = 128
PEERS = 64
ROWS = SPEC * NODES
SIGNS = (-1.0, 1.0, -1.0, 1.0, -1.0, 1.0)

INTERIOR = [i + 4 * j + 16 * k for k in (1, 2) for j in (1, 2) for i in (1, 2)]
SURFACE = [n for n in range(NODES) if n not in INTERIOR]
PLACE = {n: r for r, n in enumerate(SURFACE)}
WIDE = 16 * len(SURFACE)
GROUPS = 4
GROUP = PEERS // GROUPS


def face_node(face, first, second):
    fixed = 3 * (face % 2)
    if face < 2:
        return fixed + 4 * first + 16 * second
    if face < 4:
        return first + 4 * fixed + 16 * second
    return first + 4 * second + 16 * fixed


def rotated(quarter, index):
    a, c = index % 4, index // 4
    a, c = [(a, c), (c, 3 - a), (3 - a, 3 - c), (3 - c, a)][quarter]
    return a + 4 * c


def z_rank(dz):
    return 0 if dz == 0 else (2 * dz - 1 if dz <= 4 else 16 - 2 * dz)


def slot_of(dz, dx, dc):
    return z_rank(dz) * 8 + dx * 2 + dc


OFFSETS = sorted(
    [(a, b, d) for a in range(NZ) for b in range(NX) for d in range(2) if (a, b, d) != (0, 0, 0)],
    key=lambda o: (slot_of(*o) // GROUP, o[1], o[2], o[0]),
)


def iota(shape, dim):
    return lax.broadcasted_iota(jnp.int32, shape, dim)


def onehot(condition):
    return jnp.where(condition, 1.0, 0.0).astype(BF16)


def dot(a, b):
    return jnp.dot(a, b, preferred_element_type=F32)


def dot_nt(a, b):
    return lax.dot_general(a, b, (((1,), (1,)), ((), ())), preferred_element_type=F32)


def split(a):
    high = a.astype(BF16)
    return high, (a - high.astype(F32)).astype(BF16)


def kernel(
    cur, prev, vel, der, lift, sto, tiles, nbr, ori, lev, cnt,
    out,
    xhi, xlo, pack, land, landt, sat, hot, own_hot, grab, jump, kron, mix, ops,
    a2a_send, a2a_recv, ring_send, ring_recv,
):
    me = lax.axis_index("elem")
    y = lax.axis_index("spec")
    z, x, c = me // 8, (me // 2) % 4, me % 2
    up = (y + 1) % NY
    down = (y + NY - 1) % NY

    def plane(offset):
        a, b, d = offset
        return ((z + a) % NZ) * 8 + ((x + b) % NX) * 2 + (c + d) % 2

    barrier = pltpu.get_barrier_semaphore()
    for side in (up, down):
        pl.semaphore_signal(barrier, inc=1, device_id=(me, side), device_id_type=MESH)
    for offset in reversed(OFFSETS):
        pl.semaphore_signal(barrier, inc=1, device_id=(plane(offset), y), device_id_type=MESH)

    spread = onehot(iota((32, ELEM), 0) == iota((32, ELEM), 1) // 4)
    counts = dot(jnp.broadcast_to(cnt[...].astype(F32), (8, 32)).astype(BF16), spread)[0:1]
    alive = jnp.where((iota((1, ELEM), 1) % 4).astype(F32) < counts, 1.0, 0.0)

    def per_node(n, carry):
        value = cur[pl.ds(n, SPEC, stride=NODES), :] * alive
        rows = pl.ds(pl.multiple_of(n * SPEC, SPEC), SPEC)
        high, low = split(value)
        xhi[rows, :] = high
        xlo[rows, :] = low
        sat[0, rows, :] = (value / (1.0 + jnp.abs(value))).astype(BF16)
        return carry

    lax.fori_loop(0, NODES, per_node, 0, unroll=8)

    row = iota((PEERS * 8, 1), 0)
    expand = onehot(iota((PEERS * 8, PEERS), 0) // 8 == iota((PEERS * 8, PEERS), 1))
    chosen = dot(expand, jnp.maximum(tiles[...], 0).astype(F32).astype(BF16))
    column = jnp.where((row // 4) % 2 == 0, chosen[:, 0:1], chosen[:, 1:2])
    column = column.astype(jnp.int32) * 4 + row % 4
    select = onehot(iota((PEERS * 8, ELEM), 1) == column)
    runs = [(0, 21), (23, 25), (27, 37), (39, 41), (43, 64)]
    surface = jnp.concatenate([xhi[16 * a:16 * b, :] for a, b in runs], axis=0)
    pack[...] = dot_nt(select, surface).reshape(PEERS, 8, WIDE).astype(BF16)

    pl.semaphore_wait(barrier, len(OFFSETS) + 2)

    def ring(direction, hop, piece):
        if direction == 0:
            source, target, side = hop - 1, hop, up
        else:
            source, target, side = (8 - (hop - 1)) % 8, 8 - hop, down
        rows = pl.ds(256 * piece, 256)
        return pltpu.make_async_remote_copy(
            src_ref=sat.at[source, rows],
            dst_ref=sat.at[target, rows],
            send_sem=ring_send.at[direction, hop - 1, piece],
            recv_sem=ring_recv.at[direction, hop - 1, piece],
            device_id=(me, side),
            device_id_type=MESH,
        )

    hops = {(0, 0): 4, (0, 1): 4, (0, 2): 3, (0, 3): 3, (1, 0): 3, (1, 1): 3, (1, 2): 4, (1, 3): 4}
    order = {0: (0, 1, 2, 3), 1: (2, 3, 0, 1)}
    for k in range(4):
        for direction in (0, 1):
            ring(direction, 1, order[direction][k]).start()

    def block(offset):
        a, b, d = offset
        peer = plane(offset)
        slot = slot_of((NZ - a) % NZ, (NX - b) % NX, d)
        return pltpu.make_async_remote_copy(
            src_ref=pack.at[peer],
            dst_ref=land.at[slot],
            send_sem=a2a_send,
            recv_sem=a2a_recv.at[slot // GROUP],
            device_id=(peer, y),
            device_id_type=MESH,
        )

    for offset in OFFSETS:
        block(offset).start()
    land[0] = pack[me]

    level = lev[...]
    scale = 0.05 * alive * jnp.where(level == 0, 1.0, jnp.where(level == 1, 2.0, 4.0))
    inflow = [scale * jnp.minimum(SIGNS[f] * vel[f // 2:f // 2 + 1, :], 0.0) for f in range(6)]
    reacting = 0.05 * alive

    lift_high, lift_low = split(lift[...])
    der_high, der_low = split(der[...])
    highs, lows = [der_high.astype(F32)], [der_low.astype(F32)]
    for f in range(6):
        m, n = iota((16, NODES), 0), iota((16, NODES), 1)
        trace = onehot(n == face_node(f, m % 4, m // 4))
        highs.append(dot(lift_high[:, 16 * f:16 * f + 16], trace))
        lows.append(dot(lift_low[:, 16 * f:16 * f + 16], trace))
    high = jnp.concatenate(highs, axis=0)
    low = jnp.concatenate(lows, axis=0)
    ops[...] = jnp.concatenate([high, low, high], axis=1).astype(BF16)

    def per_species(s, carry):
        rows = pl.ds(pl.multiple_of(s * NODES, NODES), NODES)
        value = cur[rows, :] * alive
        high, low = split(value)
        terms = dot(ops[...], jnp.concatenate([high, high, low], axis=0))
        total = 0.75 * alive * prev[rows, :] + 0.25 * value
        for d in range(3):
            total = total - (scale * vel[d:d + 1, :]) * terms[64 * d:64 * d + 64]
        for f in range(6):
            total = total + inflow[f] * terms[192 + 64 * f:256 + 64 * f]
        out[rows, :] = total
        return carry

    def build_mix():
        pick = onehot(iota((256, 128), 1) == y * SPEC + iota((256, 128), 0) // 16)
        weights = dot_nt(pick, sto[...]).astype(BF16)
        keep = iota((256, 256), 0) % 16 == iota((256, 256), 1) // 16
        for o in range(NY):
            owner = (y + NY - o) % NY
            fan = onehot(iota((128, 256), 0) == owner * SPEC + iota((128, 256), 1) % 16)
            mix[o] = jnp.where(keep, dot(weights, fan), 0.0).astype(BF16)

    def react(o, piece):
        rates = dot(mix[o], sat[o, pl.ds(256 * piece, 256), :])
        for j in range(SPEC):
            rows = pl.ds(NODES * j + 16 * piece, 16)
            out[rows, :] += reacting * rates[16 * j:16 * j + 16]

    def build_hot():
        far = nbr[...] - ELEM
        peer = far >> 3
        dz = ((peer >> 3) - z) & 7
        dx = ((peer >> 1) - x) & 3
        dc = (peer + c) & 1
        rank = jnp.maximum(jnp.where(dz <= 4, 2 * dz - 1, 16 - 2 * dz), 0)
        target = jnp.where(far >= 0, rank * 64 + dx * 16 + dc * 8 + (far & 7), -1)
        for f in range(6):
            own_hot[f] = onehot(iota((ELEM, ELEM), 0) == nbr[f:f + 1, :])
            for g in range(GROUPS):
                hot[f, g] = onehot(iota((ELEM, ELEM), 0) + g * ELEM == target[f:f + 1, :])

    def far_nodes(f):
        return [face_node(f ^ 1, m % 4, m // 4) for m in range(16)]

    def take_own():
        for f in range(6):
            upper = jnp.concatenate([xhi[16 * n:16 * n + 16, :] for n in far_nodes(f)], axis=0)
            lower = jnp.concatenate([xlo[16 * n:16 * n + 16, :] for n in far_nodes(f)], axis=0)
            grab[f] = dot(upper, own_hot[f]) + dot(lower, own_hot[f])

    def take_group(g):
        arrived = land.at[pl.ds(GROUP * g, GROUP)] if g else land.at[pl.ds(1, GROUP - 1)]
        pltpu.make_async_copy(arrived, arrived, a2a_recv.at[g]).wait()
        landt[...] = land[GROUP * g:GROUP * (g + 1)].astype(F32).reshape(8 * GROUP, WIDE).T.astype(BF16)
        for f in range(6):
            places = [16 * PLACE[n] for n in far_nodes(f)]
            picked = jnp.concatenate([landt[r:r + 16, :] for r in places], axis=0)
            grab[f] += dot(picked, hot[f, g])

    def build_kron():
        fan = onehot(iota((96, 1536), 0) == iota((96, 1536), 1) // 16)
        wide = dot(lift_high, fan)
        lane = iota((NODES, 1536), 1) % 16
        for s in range(SPEC):
            kron[NODES * s:NODES * s + NODES, :] = jnp.where(lane == s, wide, 0.0).astype(BF16)

    def turn_and_lift():
        for f in range(6):
            turn = ori[f:f + 1, :]
            for m in range(16):
                source = [grab[f, 16 * rotated(q, m):16 * rotated(q, m) + 16, :] for q in range(4)]
                value = jnp.where(
                    turn < 2,
                    jnp.where(turn == 0, source[0], source[1]),
                    jnp.where(turn == 2, source[2], source[3]),
                )
                r = 256 * f + 16 * m
                jump[r:r + 16, :] = (-inflow[f] * value).astype(BF16)
        for s in range(0, SPEC, 4):
            rows = slice(NODES * s, NODES * (s + 4))
            out[rows, :] += dot(kron[rows, :], jump[...])

    def turn_ring(hop, k):
        for direction in (0, 1):
            piece = order[direction][k]
            if hop <= hops[direction, piece]:
                ring(direction, hop, piece).wait_recv()
                if hop < hops[direction, piece]:
                    ring(direction, hop + 1, piece).start()

    def react_ring(hop, k):
        for direction in (0, 1):
            piece = order[direction][k]
            if hop <= hops[direction, piece]:
                react(hop if direction == 0 else 8 - hop, piece)

    build_mix()
    lax.fori_loop(0, SPEC // 2, per_species, 0)
    turn_ring(1, 0)
    lax.fori_loop(SPEC // 2, SPEC, per_species, 0)
    turn_ring(1, 1)
    build_hot()
    turn_ring(1, 2)
    take_own()
    turn_ring(1, 3)
    build_kron()
    for piece in range(4):
        react(0, piece)
    for k in range(4):
        turn_ring(2, k)
        react_ring(1, k)
    take_group(0)
    for k in range(4):
        turn_ring(3, k)
        react_ring(2, k)
    take_group(1)
    for k in range(2):
        turn_ring(4, k)
        react_ring(3, k)
    for k in range(2, 4):
        react_ring(3, k)
    take_group(2)
    for k in range(2):
        react_ring(4, k)
    take_group(3)
    turn_and_lift()

    sent = pack.at[pl.ds(0, PEERS - 1)]
    pltpu.make_async_copy(sent, sent, a2a_send).wait()
    for (direction, piece), last in hops.items():
        for hop in range(1, last + 1):
            ring(direction, hop, piece).wait_send()


def per_device(cur, prev, vel, der, lift, sto, tiles, nbr, ori, lev, cnt):
    vmem = pl.BlockSpec(memory_space=pltpu.VMEM)
    result = pl.pallas_call(
        kernel,
        out_shape=jax.ShapeDtypeStruct((ROWS, ELEM), F32),
        in_specs=[vmem] * 11,
        out_specs=vmem,
        scratch_shapes=[
            pltpu.VMEM((ROWS, ELEM), BF16),
            pltpu.VMEM((ROWS, ELEM), BF16),
            pltpu.VMEM((PEERS, 8, WIDE), BF16),
            pltpu.VMEM((PEERS, 8, WIDE), BF16),
            pltpu.VMEM((WIDE, 8 * GROUP), BF16),
            pltpu.VMEM((NY, ROWS, ELEM), BF16),
            pltpu.VMEM((6, GROUPS, 8 * GROUP, ELEM), BF16),
            pltpu.VMEM((6, ELEM, ELEM), BF16),
            pltpu.VMEM((6, 256, ELEM), F32),
            pltpu.VMEM((1536, ELEM), BF16),
            pltpu.VMEM((ROWS, 1536), BF16),
            pltpu.VMEM((NY, 256, 256), BF16),
            pltpu.VMEM((576, 192), BF16),
            pltpu.SemaphoreType.DMA,
            pltpu.SemaphoreType.DMA((GROUPS,)),
            pltpu.SemaphoreType.DMA((2, 4, 4)),
            pltpu.SemaphoreType.DMA((2, 4, 4)),
        ],
        compiler_params=pltpu.CompilerParams(
            collective_id=0, has_side_effects=True, vmem_limit_bytes=48 * 1024 * 1024
        ),
    )(
        cur.reshape(ROWS, ELEM),
        prev.reshape(ROWS, ELEM),
        vel,
        der.reshape(3 * NODES, NODES),
        lift,
        sto,
        tiles.reshape(PEERS, 2),
        nbr,
        ori,
        lev.reshape(1, ELEM),
        cnt.reshape(1, 32),
    )
    return result.reshape(SPEC, NODES, ELEM)


def solution(mesh):
    placed = (
        P("spec", None, "elem"),
        P("spec", None, "elem"),
        P(None, "elem"),
        P(),
        P(),
        P(),
        P("elem", None, None),
        P(None, "elem"),
        P(None, "elem"),
        P("elem"),
        P("elem"),
    )
    return jax.shard_map(
        per_device, mesh=mesh, in_specs=placed, out_specs=P("spec", None, "elem"), check_vma=False
    )
```

time: 139 us -> 46 us (0.33)
  local copies, waits for them, and re-layouts: 67.4 us -> 5.37 us
  Pallas kernels: 0 us -> 40.2 us
  waiting for transfers between devices: 19.6 us -> 0 us
  starting transfers between devices: 15.2 us -> 0 us
  between operations: 14 us -> 0.09 us
  matrix products: 13.3 us -> 0 us
  other arithmetic: 8.46 us -> 0 us
    pallas_call x0 -> x1, Pallas kernels: none -> 40.2 us  [per_device(): pl.pallas_call(kernel, out_shape=jax.ShapeDtypeStruct((ROWS, ELEM), F32),...]
    gather x13 -> x0, local copies, waits for them, and re-layouts: 32.8 us -> none  [the longest x12 31.8 us: transport(): picked = jnp.take(far_traces[:, face_index], partner, axis=2)]
    unnamed x70 -> x21, local copies, waits for them, and re-layouts: 31.3 us -> 4.55 us
    all_to_all x1 -> x0, waiting for transfers between devices: 19.6 us -> none  [per_device(): lax.all_to_all(outgoing.astype(jnp.bfloat16), 'elem', split_axis=2, conca...]
    all_to_all x1 -> x0, starting transfers between devices: 15.2 us -> none  [per_device(): lax.all_to_all(outgoing.astype(jnp.bfloat16), 'elem', split_axis=2, conca...]
    dot_general x10 -> x0, matrix products: 13.3 us -> none  [the longest x4 3.29 us: transport(): jnp.einsum('xy,sfye->sfxe', jnp.asarray(rotations[quarter]), outer_trace,...]
    convert_element_type x3 -> x0, other arithmetic: 3.96 us -> none  [the longest x1 2.79 us: per_device(): outgoing.astype(jnp.bfloat16)]
    slice x1 -> x0, local copies, waits for them, and re-layouts: 1.47 us -> none  [transport(): picked = jnp.take(far_traces[:, face_index], partner, axis=2)]
  transfers between devices with their start and end apart: 2 -> 0, of which waited for: 1 -> 0; matrix products, arithmetic and copies ran while one was open for 53% -> 0% of each run, Pallas kernels for 0% -> 0%
where the time goes in v1:
time: 46 us; the launch traced here: 45.7 us
  Pallas kernels  40.2 us (87%)
  local copies, waits for them, and re-layouts  5.37 us (12%)
    pallas_call x1, Pallas kernels, per_device(): pl.pallas_call(kernel, out_shape=jax.ShapeDtypeStruct((ROWS, ELEM), F32),...  40.2 us
    unnamed x21, local copies, waits for them, and re-layouts  4.55 us

profile of v1, /device:TPU:1, one launch (start us, length us, event | category | flops | bytes accessed | tf_op | source)
XLA Modules:
  0.0 45.7 jit_solution(12665365506965094741)
XLA Ops:
  0.0 0.0 copy-start.3
  0.0 0.0 copy-start.5
  0.0 0.0 copy-start.6
  0.0 0.0 copy-start.7
  0.0 0.0 copy-start.8
  0.0 0.0 copy-start.9
  0.0 0.8 %copy.12.tiles = s32[64,2]{1,0:T(8,128)S(1)} copy(s32[64,2]{0,1:T(2,128)} %bitcast.13) | data formatting | bytes 1024 | tf_op jit(solution)/shard_map/reshape | solution.py:355
  0.9 0.0 copy-done.3
  0.9 0.0 copy-done.5
  0.9 0.0 copy-done.6
  0.9 0.0 copy-done.7
  0.9 0.0 copy-done.8
  0.9 0.0 copy-done.9
  0.9 0.0 copy-start
  0.9 1.0 %copy-done = f32[16,64,128]{2,1,0:T(8,128)S(1)} copy-done((f32[16,64,128]{2,1,0:T(8,128)S(1)}, f32[16,64,128]{2,1,0:T(8,128)}, u32[]{:S(2)}) %copy-start) | copy-done | bytes 524312
  2.0 0.0 copy-start.1
  2.0 1.0 %copy-done.1 = f32[16,64,128]{2,1,0:T(8,128)S(1)} copy-done((f32[16,64,128]{2,1,0:T(8,128)S(1)}, f32[16,64,128]{2,1,0:T(8,128)}, u32[]{:S(2)}) %copy-start.1) | copy-done | bytes 524312
  3.0 0.0 copy-start.2
  3.0 0.9 %copy-done.2 = f32[3,64,64]{2,1,0:T(8,128)S(1)} copy-done((f32[3,64,64]{2,1,0:T(8,128)S(1)}, f32[3,64,64]{2,1,0:T(8,128)}, u32[]{:S(2)}) %copy-start.2) | copy-done | bytes 49176
  3.9 0.0 copy-start.4
  3.9 0.8 %copy-done.4 = bf16[128,128]{1,0:T(8,128)(2,1)S(1)} copy-done((bf16[128,128]{1,0:T(8,128)(2,1)S(1)}, bf16[128,128]{1,0:T(8,128)(2,1)}, u32[]{:S(2)}) %copy-start.4) | copy-done | bytes 32792
  4.7 40.2 %shard_map.109 = f32[1024,128]{1,0:T(8,128)S(1)} custom-call(f32[1024,128]{1,0:T(8,128)S(1)} %bitcast.8, f32[1024,128]{1,0:T(8,128)S(1)} %bitcast.9, f32[3,128]{1,0:T(4,128)S(1)} %copy-done.7, f32[192,64]{1,0:T(8,128)S(1)} %bitcast.10, f32[64,96]{1,0:T(8,128)S(1)} %copy-done.3, bf16[128,128]{1,0:T(8,128)(2,1)S(1)} %copy-done.4, s32[64,2]{1,0:T(8,128)S(1)} %copy.12.tiles, ...), custom_call_target="tpu_custom_call" | custom-call | tf_op jit(solution)/shard_map/pallas_call | solution.py:321
  44.9 0.8 %copy.14 = f32[16,64,128]{2,1,0:T(8,128)} copy(f32[16,64,128]{2,1,0:T(8,128)S(1)} %bitcast.7) | data formatting | bytes 1048576
Async XLA Ops:
  0.0 0.9 %copy-start.3 = (f32[64,96]{1,0:T(8,128)S(1)}, f32[64,96]{1,0:T(8,128)}, u32[]{:S(2)}) copy-start(f32[64,96]{1,0:T(8,128)} %lift.1) | copy-start | bytes 73732
  0.0 0.9 %copy-start.5 = (s32[6,128]{1,0:T(8,128)S(1)}, s32[6,128]{1,0:T(8,128)}, u32[]{:S(2)}) copy-start(s32[6,128]{1,0:T(8,128)} %nbr.1) | copy-start | bytes 9220
  0.0 0.9 %copy-start.6 = (s32[6,128]{1,0:T(8,128)S(1)}, s32[6,128]{1,0:T(8,128)}, u32[]{:S(2)}) copy-start(s32[6,128]{1,0:T(8,128)} %ori.1) | copy-start | bytes 9220
  0.0 0.9 %copy-start.7 = (f32[3,128]{1,0:T(4,128)S(1)}, f32[3,128]{1,0:T(4,128)}, u32[]{:S(2)}) copy-start(f32[3,128]{1,0:T(4,128)} %vel.1) | copy-start | bytes 4612
  0.0 0.9 %copy-start.8 = (s32[128]{0:T(128)S(1)}, s32[128]{0:T(128)}, u32[]{:S(2)}) copy-start(s32[128]{0:T(128)} %param.20) | copy-start | bytes 1540
  0.0 0.9 %copy-start.9 = (s32[32]{0:T(128)S(1)}, s32[32]{0:T(128)}, u32[]{:S(2)}) copy-start(s32[32]{0:T(128)} %param.21) | copy-start | bytes 388
  0.9 1.0 %copy-start = (f32[16,64,128]{2,1,0:T(8,128)S(1)}, f32[16,64,128]{2,1,0:T(8,128)}, u32[]{:S(2)}) copy-start(f32[16,64,128]{2,1,0:T(8,128)} %param.11) | copy-start | bytes 1572868
  2.0 1.0 %copy-start.1 = (f32[16,64,128]{2,1,0:T(8,128)S(1)}, f32[16,64,128]{2,1,0:T(8,128)}, u32[]{:S(2)}) copy-start(f32[16,64,128]{2,1,0:T(8,128)} %param.12) | copy-start | bytes 1572868
  3.0 0.9 %copy-start.2 = (f32[3,64,64]{2,1,0:T(8,128)S(1)}, f32[3,64,64]{2,1,0:T(8,128)}, u32[]{:S(2)}) copy-start(f32[3,64,64]{2,1,0:T(8,128)} %param.14) | copy-start | bytes 147460
  3.9 0.8 %copy-start.4 = (bf16[128,128]{1,0:T(8,128)(2,1)S(1)}, bf16[128,128]{1,0:T(8,128)(2,1)}, u32[]{:S(2)}) copy-start(bf16[128,128]{1,0:T(8,128)(2,1)} %sto.1) | copy-start | bytes 98308

commit v2 on v1

--- a/solution.py
+++ b/solution.py
@@ -1,5 +1,3 @@
-import functools
-
 import jax
 import jax.numpy as jnp
 import numpy as np
@@ -53,8 +51,10 @@
 
 OFFSETS = sorted(
     [(a, b, d) for a in range(NZ) for b in range(NX) for d in range(2) if (a, b, d) != (0, 0, 0)],
-    key=lambda o: (slot_of(*o) // GROUP, o[1], o[2], o[0]),
+    key=lambda o: (min(o[0], NZ - o[0]), o[1], o[2], o[0]),
 )
+ROW = [o for o in OFFSETS if o[0] == 0]
+COLUMN = [o for o in OFFSETS if o[1:] == (0, 0)]
 
 
 def iota(shape, dim):
@@ -79,10 +79,11 @@
 
 
 def kernel(
+    cur_in, prev_in, vel_in, der_in, lift_in, sto_in, tiles_in, nbr_in, ori_in, lev_in, cnt_in,
+    out,
     cur, prev, vel, der, lift, sto, tiles, nbr, ori, lev, cnt,
-    out,
-    xhi, xlo, pack, land, landt, sat, hot, own_hot, grab, jump, kron, mix, ops,
-    a2a_send, a2a_recv, ring_send, ring_recv,
+    xhi, xlo, pack, land, landt, sat, hot, own_hot, grab, jump, mix, ops,
+    in_sem, a2a_send, a2a_recv, ring_send, ring_recv, ready,
 ):
     me = lax.axis_index("elem")
     y = lax.axis_index("spec")
@@ -94,15 +95,30 @@
         a, b, d = offset
         return ((z + a) % NZ) * 8 + ((x + b) % NX) * 2 + (c + d) % 2
 
+    loads = [
+        pltpu.make_async_copy(source, target, in_sem.at[k])
+        for k, (source, target) in enumerate([
+            (cur_in, cur), (cnt_in, cnt), (tiles_in, tiles), (vel_in, vel), (lev_in, lev), (lift_in, lift),
+            (der_in, der), (sto_in, sto), (nbr_in, nbr), (ori_in, ori), (prev_in, prev),
+        ])
+    ]
+    for load in loads:
+        load.start()
+
     barrier = pltpu.get_barrier_semaphore()
+    for offset in reversed(COLUMN):
+        pl.semaphore_signal(barrier, inc=1, device_id=(plane(offset), y), device_id_type=MESH)
     for side in (up, down):
         pl.semaphore_signal(barrier, inc=1, device_id=(me, side), device_id_type=MESH)
-    for offset in reversed(OFFSETS):
+    for offset in ROW:
         pl.semaphore_signal(barrier, inc=1, device_id=(plane(offset), y), device_id_type=MESH)
+    loads[1].wait()
 
     spread = onehot(iota((32, ELEM), 0) == iota((32, ELEM), 1) // 4)
     counts = dot(jnp.broadcast_to(cnt[...].astype(F32), (8, 32)).astype(BF16), spread)[0:1]
     alive = jnp.where((iota((1, ELEM), 1) % 4).astype(F32) < counts, 1.0, 0.0)
+
+    loads[0].wait()
 
     def per_node(n, carry):
         value = cur[pl.ds(n, SPEC, stride=NODES), :] * alive
@@ -114,18 +130,6 @@
         return carry
 
     lax.fori_loop(0, NODES, per_node, 0, unroll=8)
-
-    row = iota((PEERS * 8, 1), 0)
-    expand = onehot(iota((PEERS * 8, PEERS), 0) // 8 == iota((PEERS * 8, PEERS), 1))
-    chosen = dot(expand, jnp.maximum(tiles[...], 0).astype(F32).astype(BF16))
-    column = jnp.where((row // 4) % 2 == 0, chosen[:, 0:1], chosen[:, 1:2])
-    column = column.astype(jnp.int32) * 4 + row % 4
-    select = onehot(iota((PEERS * 8, ELEM), 1) == column)
-    runs = [(0, 21), (23, 25), (27, 37), (39, 41), (43, 64)]
-    surface = jnp.concatenate([xhi[16 * a:16 * b, :] for a, b in runs], axis=0)
-    pack[...] = dot_nt(select, surface).reshape(PEERS, 8, WIDE).astype(BF16)
-
-    pl.semaphore_wait(barrier, len(OFFSETS) + 2)
 
     def ring(direction, hop, piece):
         if direction == 0:
@@ -144,6 +148,24 @@
 
     hops = {(0, 0): 4, (0, 1): 4, (0, 2): 3, (0, 3): 3, (1, 0): 3, (1, 1): 3, (1, 2): 4, (1, 3): 4}
     order = {0: (0, 1, 2, 3), 1: (2, 3, 0, 1)}
+    loads[2].wait()
+    row = iota((PEERS * 8, 1), 0)
+    expand = onehot(iota((PEERS * 8, PEERS), 0) // 8 == iota((PEERS * 8, PEERS), 1))
+    listed = jnp.maximum(tiles[...], 0).astype(F32)
+    listed = jnp.concatenate(
+        [jnp.broadcast_to(listed[0:1], (8, PEERS)), jnp.broadcast_to(listed[1:2], (8, PEERS))], axis=0
+    ).astype(BF16)
+    chosen = dot_nt(expand, listed)
+    column = jnp.where((row // 4) % 2 == 0, chosen[:, 0:1], chosen[:, 8:9])
+    column = column.astype(jnp.int32) * 4 + row % 4
+    select = onehot(iota((PEERS * 8, ELEM), 1) == column)
+    runs = [(0, 21), (23, 25), (27, 37), (39, 41), (43, 64)]
+    surface = jnp.concatenate([xhi[16 * a:16 * b, :] for a, b in runs], axis=0)
+    pack[...] = dot_nt(select, surface).reshape(PEERS, 8, WIDE).astype(BF16)
+
+    pl.semaphore_wait(barrier, len(ROW) + len(COLUMN) + 2)
+    for offset in ROW:
+        pl.semaphore_signal(ready, inc=1, device_id=(plane(offset), y), device_id_type=MESH)
     for k in range(4):
         for direction in (0, 1):
             ring(direction, 1, order[direction][k]).start()
@@ -161,38 +183,60 @@
             device_id_type=MESH,
         )
 
+    for offset in COLUMN + ROW:
+        block(offset).start()
+    pl.semaphore_wait(ready, len(ROW))
     for offset in OFFSETS:
-        block(offset).start()
+        if offset not in COLUMN + ROW:
+            block(offset).start()
     land[0] = pack[me]
 
+    def turn_ring(hop, k):
+        for direction in (0, 1):
+            piece = order[direction][k]
+            if hop <= hops[direction, piece]:
+                ring(direction, hop, piece).wait_recv()
+                if hop < hops[direction, piece]:
+                    ring(direction, hop + 1, piece).start()
+
+    for load in loads[3:]:
+        load.wait()
     level = lev[...]
     scale = 0.05 * alive * jnp.where(level == 0, 1.0, jnp.where(level == 1, 2.0, 4.0))
     inflow = [scale * jnp.minimum(SIGNS[f] * vel[f // 2:f // 2 + 1, :], 0.0) for f in range(6)]
     reacting = 0.05 * alive
 
     lift_high, lift_low = split(lift[...])
-    der_high, der_low = split(der[...])
-    highs, lows = [der_high.astype(F32)], [der_low.astype(F32)]
-    for f in range(6):
-        m, n = iota((16, NODES), 0), iota((16, NODES), 1)
-        trace = onehot(n == face_node(f, m % 4, m // 4))
-        highs.append(dot(lift_high[:, 16 * f:16 * f + 16], trace))
-        lows.append(dot(lift_low[:, 16 * f:16 * f + 16], trace))
-    high = jnp.concatenate(highs, axis=0)
-    low = jnp.concatenate(lows, axis=0)
-    ops[...] = jnp.concatenate([high, low, high], axis=1).astype(BF16)
-
-    def per_species(s, carry):
-        rows = pl.ds(pl.multiple_of(s * NODES, NODES), NODES)
-        value = cur[rows, :] * alive
+
+    def build_ops():
+        der_high, der_low = split(der[...])
+        highs, lows = [der_high.astype(F32)], [der_low.astype(F32)]
+        for f in range(6):
+            m, n = iota((16, NODES), 0), iota((16, NODES), 1)
+            trace = onehot(n == face_node(f, m % 4, m // 4))
+            highs.append(dot(lift_high[:, 16 * f:16 * f + 16], trace))
+            lows.append(dot(lift_low[:, 16 * f:16 * f + 16], trace))
+        high = jnp.concatenate(highs, axis=0)
+        low = jnp.concatenate(lows, axis=0)
+        ops[...] = jnp.concatenate([high, low, high], axis=1).astype(BF16)
+
+    def twice(a):
+        return jnp.concatenate([a, a], axis=1)
+
+    def per_pair(s, carry):
+        first = pl.ds(pl.multiple_of(2 * s * NODES, NODES), NODES)
+        second = pl.ds(pl.multiple_of((2 * s + 1) * NODES, NODES), NODES)
+        value = jnp.concatenate([cur[first, :], cur[second, :]], axis=1) * twice(alive)
+        old = jnp.concatenate([prev[first, :], prev[second, :]], axis=1)
         high, low = split(value)
-        terms = dot(ops[...], jnp.concatenate([high, high, low], axis=0))
-        total = 0.75 * alive * prev[rows, :] + 0.25 * value
+        right = jnp.concatenate([high, high, low], axis=0)
+        total = twice(0.75 * alive) * old + 0.25 * value
         for d in range(3):
-            total = total - (scale * vel[d:d + 1, :]) * terms[64 * d:64 * d + 64]
-        for f in range(6):
-            total = total + inflow[f] * terms[192 + 64 * f:256 + 64 * f]
-        out[rows, :] = total
+            total -= twice(scale * vel[d:d + 1, :]) * dot(ops[64 * d:64 * d + 64, :], right)
+        for f in range(6):
+            total += twice(inflow[f]) * dot(ops[192 + 64 * f:256 + 64 * f, :], right)
+        out[first, :] = total[:, :ELEM]
+        out[second, :] = total[:, ELEM:]
         return carry
 
     def build_mix():
@@ -204,11 +248,17 @@
             fan = onehot(iota((128, 256), 0) == owner * SPEC + iota((128, 256), 1) % 16)
             mix[o] = jnp.where(keep, dot(weights, fan), 0.0).astype(BF16)
 
-    def react(o, piece):
-        rates = dot(mix[o], sat[o, pl.ds(256 * piece, 256), :])
+    def react(o, half):
+        left, right = 2 * half, 2 * half + 1
+        states = jnp.concatenate(
+            [sat[o, 256 * left:256 * left + 256, :], sat[o, 256 * right:256 * right + 256, :]], axis=1
+        )
+        rates = dot(mix[o], states)
         for j in range(SPEC):
-            rows = pl.ds(NODES * j + 16 * piece, 16)
-            out[rows, :] += reacting * rates[16 * j:16 * j + 16]
+            rows = pl.ds(NODES * j + 16 * left, 16)
+            out[rows, :] += reacting * rates[16 * j:16 * j + 16, :ELEM]
+            rows = pl.ds(NODES * j + 16 * right, 16)
+            out[rows, :] += reacting * rates[16 * j:16 * j + 16, ELEM:]
 
     def build_hot():
         far = nbr[...] - ELEM
@@ -240,13 +290,6 @@
             places = [16 * PLACE[n] for n in far_nodes(f)]
             picked = jnp.concatenate([landt[r:r + 16, :] for r in places], axis=0)
             grab[f] += dot(picked, hot[f, g])
-
-    def build_kron():
-        fan = onehot(iota((96, 1536), 0) == iota((96, 1536), 1) // 16)
-        wide = dot(lift_high, fan)
-        lane = iota((NODES, 1536), 1) % 16
-        for s in range(SPEC):
-            kron[NODES * s:NODES * s + NODES, :] = jnp.where(lane == s, wide, 0.0).astype(BF16)
 
     def turn_and_lift():
         for f in range(6):
@@ -259,53 +302,57 @@
                     jnp.where(turn == 2, source[2], source[3]),
                 )
                 r = 256 * f + 16 * m
-                jump[r:r + 16, :] = (-inflow[f] * value).astype(BF16)
-        for s in range(0, SPEC, 4):
-            rows = slice(NODES * s, NODES * (s + 4))
-            out[rows, :] += dot(kron[rows, :], jump[...])
-
-    def turn_ring(hop, k):
-        for direction in (0, 1):
-            piece = order[direction][k]
-            if hop <= hops[direction, piece]:
-                ring(direction, hop, piece).wait_recv()
-                if hop < hops[direction, piece]:
-                    ring(direction, hop + 1, piece).start()
-
-    def react_ring(hop, k):
-        for direction in (0, 1):
-            piece = order[direction][k]
-            if hop <= hops[direction, piece]:
-                react(hop if direction == 0 else 8 - hop, piece)
-
+                jump[r:r + 16, :] = -inflow[f] * value
+        for s in range(0, SPEC, 2):
+            pair = [jump[pl.ds(s + t, 96, stride=SPEC), :] for t in range(2)]
+            lifted = dot(lift_high, jnp.concatenate(pair, axis=1).astype(BF16))
+            out[NODES * s:NODES * s + NODES, :] += lifted[:, :ELEM]
+            out[NODES * s + NODES:NODES * s + 2 * NODES, :] += lifted[:, ELEM:]
+
+    def react_ring(hop, half):
+        if hop <= hops[0, 2 * half]:
+            react(hop, half)
+        if hop <= hops[1, 2 * half]:
+            react(8 - hop, half)
+
+    def pairs(first, last):
+        lax.fori_loop(first, last, per_pair, 0)
+
+    build_ops()
+    turn_ring(1, 0)
+    pairs(0, 2)
+    turn_ring(1, 1)
+    pairs(2, 4)
+    turn_ring(1, 2)
+    pairs(4, 6)
+    turn_ring(1, 3)
+    pairs(6, 8)
+    turn_ring(2, 0)
     build_mix()
-    lax.fori_loop(0, SPEC // 2, per_species, 0)
-    turn_ring(1, 0)
-    lax.fori_loop(SPEC // 2, SPEC, per_species, 0)
-    turn_ring(1, 1)
+    turn_ring(2, 1)
     build_hot()
-    turn_ring(1, 2)
+    react(0, 0)
+    turn_ring(2, 2)
     take_own()
-    turn_ring(1, 3)
-    build_kron()
-    for piece in range(4):
-        react(0, piece)
-    for k in range(4):
-        turn_ring(2, k)
-        react_ring(1, k)
+    react(0, 1)
+    turn_ring(2, 3)
+    react_ring(1, 0)
+    turn_ring(3, 0)
+    react_ring(1, 1)
+    turn_ring(3, 1)
+    react_ring(2, 0)
+    turn_ring(3, 2)
+    react_ring(2, 1)
+    turn_ring(3, 3)
+    react_ring(3, 0)
     take_group(0)
-    for k in range(4):
-        turn_ring(3, k)
-        react_ring(2, k)
+    turn_ring(4, 0)
+    react_ring(3, 1)
     take_group(1)
-    for k in range(2):
-        turn_ring(4, k)
-        react_ring(3, k)
-    for k in range(2, 4):
-        react_ring(3, k)
+    turn_ring(4, 1)
+    react_ring(4, 0)
+    react_ring(4, 1)
     take_group(2)
-    for k in range(2):
-        react_ring(4, k)
     take_group(3)
     turn_and_lift()
 
@@ -317,13 +364,25 @@
 
 
 def per_device(cur, prev, vel, der, lift, sto, tiles, nbr, ori, lev, cnt):
-    vmem = pl.BlockSpec(memory_space=pltpu.VMEM)
+    operands = [
+        cur.reshape(ROWS, ELEM),
+        prev.reshape(ROWS, ELEM),
+        vel,
+        der.reshape(3 * NODES, NODES),
+        lift,
+        sto,
+        tiles[0].T,
+        nbr,
+        ori,
+        lev.reshape(1, ELEM),
+        cnt.reshape(1, 32),
+    ]
     result = pl.pallas_call(
         kernel,
         out_shape=jax.ShapeDtypeStruct((ROWS, ELEM), F32),
-        in_specs=[vmem] * 11,
-        out_specs=vmem,
-        scratch_shapes=[
+        in_specs=[pl.BlockSpec(memory_space=pltpu.HBM)] * 11,
+        out_specs=pl.BlockSpec(memory_space=pltpu.VMEM),
+        scratch_shapes=[pltpu.VMEM(operand.shape, operand.dtype) for operand in operands] + [
             pltpu.VMEM((ROWS, ELEM), BF16),
             pltpu.VMEM((ROWS, ELEM), BF16),
             pltpu.VMEM((PEERS, 8, WIDE), BF16),
@@ -333,31 +392,20 @@
             pltpu.VMEM((6, GROUPS, 8 * GROUP, ELEM), BF16),
             pltpu.VMEM((6, ELEM, ELEM), BF16),
             pltpu.VMEM((6, 256, ELEM), F32),
-            pltpu.VMEM((1536, ELEM), BF16),
-            pltpu.VMEM((ROWS, 1536), BF16),
+            pltpu.VMEM((1536, ELEM), F32),
             pltpu.VMEM((NY, 256, 256), BF16),
             pltpu.VMEM((576, 192), BF16),
+            pltpu.SemaphoreType.DMA((11,)),
             pltpu.SemaphoreType.DMA,
             pltpu.SemaphoreType.DMA((GROUPS,)),
             pltpu.SemaphoreType.DMA((2, 4, 4)),
             pltpu.SemaphoreType.DMA((2, 4, 4)),
+            pltpu.SemaphoreType.REGULAR,
         ],
         compiler_params=pltpu.CompilerParams(
-            collective_id=0, has_side_effects=True, vmem_limit_bytes=48 * 1024 * 1024
+            collective_id=0, has_side_effects=True, vmem_limit_bytes=58 * 1024 * 1024
         ),
-    )(
-        cur.reshape(ROWS, ELEM),
-        prev.reshape(ROWS, ELEM),
-        vel,
-        der.reshape(3 * NODES, NODES),
-        lift,
-        sto,
-        tiles.reshape(PEERS, 2),
-        nbr,
-        ori,
-        lev.reshape(1, ELEM),
-        cnt.reshape(1, 32),
-    )
+    )(*operands)
     return result.reshape(SPEC, NODES, ELEM)
 
 

time: 46 us -> 39.8 us (0.87)
  local copies, waits for them, and re-layouts: 5.37 us -> 1.89 us
  Pallas kernels: 40.2 us -> 37.7 us
    unnamed x21 -> x1, local copies, waits for them, and re-layouts: 4.55 us -> 1.89 us
    pallas_call x1, Pallas kernels: 40.2 us -> 37.7 us  [per_device(): pl.pallas_call(kernel, out_shape=jax.ShapeDtypeStruct((ROWS, ELEM), F32),...]
    reshape x1 -> x0, local copies, waits for them, and re-layouts: 0.82 us -> none  [per_device(): tiles.reshape(PEERS, 2)]
where the time goes in v2:
time: 39.8 us; the launch traced here: 39.6 us
  Pallas kernels  37.7 us (95%)
  local copies, waits for them, and re-layouts  1.89 us (5%)
    pallas_call x1, Pallas kernels, per_device(): pl.pallas_call(kernel, out_shape=jax.ShapeDtypeStruct((ROWS, ELEM), F32),...  37.7 us
    unnamed x1, local copies, waits for them, and re-layouts  1.89 us

profile of v2, /device:TPU:1, one launch (start us, length us, event | category | flops | bytes accessed | tf_op | source)
XLA Modules:
  0.0 39.6 jit_solution(6062940710214970882)
XLA Ops:
  0.0 37.7 %shard_map.109 = f32[1024,128]{1,0:T(8,128)} custom-call(f32[1024,128]{1,0:T(8,128)} %bitcast.10, f32[1024,128]{1,0:T(8,128)} %bitcast.11, f32[3,128]{1,0:T(4,128)} %vel_in.1, f32[192,64]{1,0:T(8,128)} %bitcast.12, f32[64,96]{1,0:T(8,128)} %lift_in.1, bf16[128,128]{1,0:T(8,128)(2,1)} %sto_in.1, s32[2,64]{1,0:T(2,128)} %bitcast.13, s32[6,128]{1,0:T(8,128)} %nbr_in.1, ...), custom_call_target="tpu_custom_call" | custom-call | tf_op jit(solution)/shard_map/pallas_call | solution.py:380
  37.7 1.9 %copy.13 = f32[16,64,128]{2,1,0:T(8,128)} copy(f32[16,64,128]{2,1,0:T(8,128)} %bitcast.9) | data formatting | bytes 1048576

commit v3 on v2

--- a/solution.py
+++ b/solution.py
@@ -41,20 +41,10 @@
     return a + 4 * c
 
 
-def z_rank(dz):
-    return 0 if dz == 0 else (2 * dz - 1 if dz <= 4 else 16 - 2 * dz)
-
-
-def slot_of(dz, dx, dc):
-    return z_rank(dz) * 8 + dx * 2 + dc
-
-
-OFFSETS = sorted(
-    [(a, b, d) for a in range(NZ) for b in range(NX) for d in range(2) if (a, b, d) != (0, 0, 0)],
-    key=lambda o: (min(o[0], NZ - o[0]), o[1], o[2], o[0]),
-)
-ROW = [o for o in OFFSETS if o[0] == 0]
-COLUMN = [o for o in OFFSETS if o[1:] == (0, 0)]
+COLUMN = [(a, 0, 0) for a in range(1, NZ)]
+ROW = [(0, b, d) for b in range(NX) for d in range(2)][1:]
+
+ORDER = [[7, 6, 5, 4, 1, 2, 3], [6, 5, 4, 3, 7, 1, 2], [2, 3, 4, 5, 6, 7, 1], [5, 6, 7, 1, 2, 3, 4], [4, 5, 6, 7, 1, 2, 3], [3, 4, 5, 6, 7, 1, 2], [2, 3, 4, 5, 6, 7, 1], [1, 2, 3, 4, 5, 6, 7]]
 
 
 def iota(shape, dim):
@@ -80,10 +70,10 @@
 
 def kernel(
     cur_in, prev_in, vel_in, der_in, lift_in, sto_in, tiles_in, nbr_in, ori_in, lev_in, cnt_in,
-    out,
-    cur, prev, vel, der, lift, sto, tiles, nbr, ori, lev, cnt,
+    result,
+    out, cur, prev, vel, der, lift, sto, tiles, nbr, ori, lev, cnt,
     xhi, xlo, pack, land, landt, sat, hot, own_hot, grab, jump, mix, ops,
-    in_sem, a2a_send, a2a_recv, ring_send, ring_recv, ready,
+    in_sem, out_sem, a2a_send, a2a_recv, ring_send, ring_recv, ready,
 ):
     me = lax.axis_index("elem")
     y = lax.axis_index("spec")
@@ -170,26 +160,29 @@
         for direction in (0, 1):
             ring(direction, 1, order[direction][k]).start()
 
-    def block(offset):
-        a, b, d = offset
-        peer = plane(offset)
-        slot = slot_of((NZ - a) % NZ, (NX - b) % NX, d)
-        return pltpu.make_async_remote_copy(
+    def send(peer):
+        pltpu.make_async_remote_copy(
             src_ref=pack.at[peer],
-            dst_ref=land.at[slot],
+            dst_ref=land.at[me],
             send_sem=a2a_send,
-            recv_sem=a2a_recv.at[slot // GROUP],
+            recv_sem=a2a_recv.at[z // 2],
             device_id=(peer, y),
             device_id_type=MESH,
-        )
-
-    for offset in COLUMN + ROW:
-        block(offset).start()
+        ).start()
+
+    pltpu.make_async_copy(pack.at[me], land.at[me], a2a_recv.at[z // 2]).start()
+    for offset in ROW:
+        send(plane(offset))
+    steps = []
+    for i in range(NZ - 1):
+        digits = sum(ORDER[r][i] << (3 * r) for r in range(NZ))
+        steps.append((digits >> (3 * z)) & 7)
+    for a in steps:
+        send(plane((a, 0, 0)))
     pl.semaphore_wait(ready, len(ROW))
-    for offset in OFFSETS:
-        if offset not in COLUMN + ROW:
-            block(offset).start()
-    land[0] = pack[me]
+    for a in steps:
+        for _, b, d in ROW:
+            send(plane((a, b, d)))
 
     def turn_ring(hop, k):
         for direction in (0, 1):
@@ -262,16 +255,10 @@
 
     def build_hot():
         far = nbr[...] - ELEM
-        peer = far >> 3
-        dz = ((peer >> 3) - z) & 7
-        dx = ((peer >> 1) - x) & 3
-        dc = (peer + c) & 1
-        rank = jnp.maximum(jnp.where(dz <= 4, 2 * dz - 1, 16 - 2 * dz), 0)
-        target = jnp.where(far >= 0, rank * 64 + dx * 16 + dc * 8 + (far & 7), -1)
         for f in range(6):
             own_hot[f] = onehot(iota((ELEM, ELEM), 0) == nbr[f:f + 1, :])
             for g in range(GROUPS):
-                hot[f, g] = onehot(iota((ELEM, ELEM), 0) + g * ELEM == target[f:f + 1, :])
+                hot[f, g] = onehot(iota((ELEM, ELEM), 0) + g * ELEM == far[f:f + 1, :])
 
     def far_nodes(f):
         return [face_node(f ^ 1, m % 4, m // 4) for m in range(16)]
@@ -283,7 +270,7 @@
             grab[f] = dot(upper, own_hot[f]) + dot(lower, own_hot[f])
 
     def take_group(g):
-        arrived = land.at[pl.ds(GROUP * g, GROUP)] if g else land.at[pl.ds(1, GROUP - 1)]
+        arrived = land.at[pl.ds(GROUP * g, GROUP)]
         pltpu.make_async_copy(arrived, arrived, a2a_recv.at[g]).wait()
         landt[...] = land[GROUP * g:GROUP * (g + 1)].astype(F32).reshape(8 * GROUP, WIDE).T.astype(BF16)
         for f in range(6):
@@ -346,21 +333,25 @@
     turn_ring(3, 3)
     react_ring(3, 0)
     take_group(0)
-    turn_ring(4, 0)
     react_ring(3, 1)
     take_group(1)
-    turn_ring(4, 1)
-    react_ring(4, 0)
-    react_ring(4, 1)
     take_group(2)
     take_group(3)
     turn_and_lift()
+    turn_ring(4, 0)
+    turn_ring(4, 1)
+    for half in range(2):
+        react(4, half)
+        for s in range(SPEC):
+            rows = pl.ds(NODES * s + 32 * half, 32)
+            pltpu.make_async_copy(out.at[rows], result.at[rows], out_sem).start()
 
     sent = pack.at[pl.ds(0, PEERS - 1)]
     pltpu.make_async_copy(sent, sent, a2a_send).wait()
     for (direction, piece), last in hops.items():
         for hop in range(1, last + 1):
             ring(direction, hop, piece).wait_send()
+    pltpu.make_async_copy(out, result, out_sem).wait()
 
 
 def per_device(cur, prev, vel, der, lift, sto, tiles, nbr, ori, lev, cnt):
@@ -381,8 +372,10 @@
         kernel,
         out_shape=jax.ShapeDtypeStruct((ROWS, ELEM), F32),
         in_specs=[pl.BlockSpec(memory_space=pltpu.HBM)] * 11,
-        out_specs=pl.BlockSpec(memory_space=pltpu.VMEM),
-        scratch_shapes=[pltpu.VMEM(operand.shape, operand.dtype) for operand in operands] + [
+        out_specs=pl.BlockSpec(memory_space=pltpu.HBM),
+        scratch_shapes=[
+            pltpu.VMEM((ROWS, ELEM), F32)
+        ] + [pltpu.VMEM(operand.shape, operand.dtype) for operand in operands] + [
             pltpu.VMEM((ROWS, ELEM), BF16),
             pltpu.VMEM((ROWS, ELEM), BF16),
             pltpu.VMEM((PEERS, 8, WIDE), BF16),
@@ -396,6 +389,7 @@
             pltpu.VMEM((NY, 256, 256), BF16),
             pltpu.VMEM((576, 192), BF16),
             pltpu.SemaphoreType.DMA((11,)),
+            pltpu.SemaphoreType.DMA,
             pltpu.SemaphoreType.DMA,
             pltpu.SemaphoreType.DMA((GROUPS,)),
             pltpu.SemaphoreType.DMA((2, 4, 4)),

time: 39.8 us -> 38.3 us (0.962)
  Pallas kernels: 37.7 us -> 35.9 us
    pallas_call x1, Pallas kernels: 37.7 us -> 35.9 us  [per_device(): pl.pallas_call(kernel, out_shape=jax.ShapeDtypeStruct((ROWS, ELEM), F32),...]
where the time goes in v3:
time: 38.3 us; the launch traced here: 37.8 us
  Pallas kernels  35.9 us (94%)
  local copies, waits for them, and re-layouts  1.89 us (5%)
    pallas_call x1, Pallas kernels, per_device(): pl.pallas_call(kernel, out_shape=jax.ShapeDtypeStruct((ROWS, ELEM), F32),...  35.9 us
    unnamed x1, local copies, waits for them, and re-layouts  1.89 us

profile of v3, /device:TPU:1, one launch (start us, length us, event | category | flops | bytes accessed | tf_op | source)
XLA Modules:
  0.0 37.8 jit_solution(18240308040148520353)
XLA Ops:
  0.0 35.9 %shard_map.109 = f32[1024,128]{1,0:T(8,128)} custom-call(f32[1024,128]{1,0:T(8,128)} %bitcast.10, f32[1024,128]{1,0:T(8,128)} %bitcast.11, f32[3,128]{1,0:T(4,128)} %vel_in.1, f32[192,64]{1,0:T(8,128)} %bitcast.12, f32[64,96]{1,0:T(8,128)} %lift_in.1, bf16[128,128]{1,0:T(8,128)(2,1)} %sto_in.1, s32[2,64]{1,0:T(2,128)} %bitcast.13, s32[6,128]{1,0:T(8,128)} %nbr_in.1, ...), custom_call_target="tpu_custom_call" | custom-call | tf_op jit(solution)/shard_map/pallas_call | solution.py:371
  35.9 1.9 %copy.13 = f32[16,64,128]{2,1,0:T(8,128)} copy(f32[16,64,128]{2,1,0:T(8,128)} %bitcast.9) | data formatting | bytes 1048576

commit v4 on v3

--- a/solution.py
+++ b/solution.py
@@ -92,16 +92,22 @@
             (der_in, der), (sto_in, sto), (nbr_in, nbr), (ori_in, ori), (prev_in, prev),
         ])
     ]
-    for load in loads:
-        load.start()
-
     barrier = pltpu.get_barrier_semaphore()
     for offset in reversed(COLUMN):
         pl.semaphore_signal(barrier, inc=1, device_id=(plane(offset), y), device_id_type=MESH)
     for side in (up, down):
         pl.semaphore_signal(barrier, inc=1, device_id=(me, side), device_id_type=MESH)
+    loads[0].start()
     for offset in ROW:
         pl.semaphore_signal(barrier, inc=1, device_id=(plane(offset), y), device_id_type=MESH)
+    for load in loads[1:]:
+        load.start()
+
+    def enter():
+        pl.semaphore_wait(barrier, len(ROW) + len(COLUMN) + 2)
+        for offset in ROW:
+            pl.semaphore_signal(ready, inc=1, device_id=(plane(offset), y), device_id_type=MESH)
+
     loads[1].wait()
 
     spread = onehot(iota((32, ELEM), 0) == iota((32, ELEM), 1) // 4)
@@ -153,9 +159,8 @@
     surface = jnp.concatenate([xhi[16 * a:16 * b, :] for a, b in runs], axis=0)
     pack[...] = dot_nt(select, surface).reshape(PEERS, 8, WIDE).astype(BF16)
 
-    pl.semaphore_wait(barrier, len(ROW) + len(COLUMN) + 2)
-    for offset in ROW:
-        pl.semaphore_signal(ready, inc=1, device_id=(plane(offset), y), device_id_type=MESH)
+    enter()
+
     for k in range(4):
         for direction in (0, 1):
             ring(direction, 1, order[direction][k]).start()
@@ -295,6 +300,8 @@
             lifted = dot(lift_high, jnp.concatenate(pair, axis=1).astype(BF16))
             out[NODES * s:NODES * s + NODES, :] += lifted[:, :ELEM]
             out[NODES * s + NODES:NODES * s + 2 * NODES, :] += lifted[:, ELEM:]
+            rows = pl.ds(NODES * s, 2 * NODES)
+            pltpu.make_async_copy(out.at[rows], result.at[rows], out_sem).start()
 
     def react_ring(hop, half):
         if hop <= hops[0, 2 * half]:
@@ -336,15 +343,12 @@
     react_ring(3, 1)
     take_group(1)
     take_group(2)
+    turn_ring(4, 0)
+    turn_ring(4, 1)
+    react(4, 0)
+    react(4, 1)
     take_group(3)
     turn_and_lift()
-    turn_ring(4, 0)
-    turn_ring(4, 1)
-    for half in range(2):
-        react(4, half)
-        for s in range(SPEC):
-            rows = pl.ds(NODES * s + 32 * half, 32)
-            pltpu.make_async_copy(out.at[rows], result.at[rows], out_sem).start()
 
     sent = pack.at[pl.ds(0, PEERS - 1)]
     pltpu.make_async_copy(sent, sent, a2a_send).wait()

time: 38.3 us -> 38 us (level)
  no operation moved by 1% of the time
where the time goes in v4:
time: 38 us; the launch traced here: 37.7 us
  Pallas kernels  35.8 us (94%)
  local copies, waits for them, and re-layouts  1.89 us (5%)
    pallas_call x1, Pallas kernels, per_device(): pl.pallas_call(kernel, out_shape=jax.ShapeDtypeStruct((ROWS, ELEM), F32),...  35.8 us
    unnamed x1, local copies, waits for them, and re-layouts  1.89 us

profile of v4, /device:TPU:1, one launch (start us, length us, event | category | flops | bytes accessed | tf_op | source)
XLA Modules:
  0.0 37.7 jit_solution(9335747120389967437)
XLA Ops:
  0.0 35.8 %shard_map.109 = f32[1024,128]{1,0:T(8,128)} custom-call(f32[1024,128]{1,0:T(8,128)} %bitcast.10, f32[1024,128]{1,0:T(8,128)} %bitcast.11, f32[3,128]{1,0:T(4,128)} %vel_in.1, f32[192,64]{1,0:T(8,128)} %bitcast.12, f32[64,96]{1,0:T(8,128)} %lift_in.1, bf16[128,128]{1,0:T(8,128)(2,1)} %sto_in.1, s32[2,64]{1,0:T(2,128)} %bitcast.13, s32[6,128]{1,0:T(8,128)} %nbr_in.1, ...), custom_call_target="tpu_custom_call" | custom-call | tf_op jit(solution)/shard_map/pallas_call | solution.py:375
  35.8 1.9 %copy.13 = f32[16,64,128]{2,1,0:T(8,128)} copy(f32[16,64,128]{2,1,0:T(8,128)} %bitcast.9) | data formatting | bytes 1048576

commit v5 on v4

--- a/solution.py
+++ b/solution.py
@@ -44,7 +44,7 @@
 COLUMN = [(a, 0, 0) for a in range(1, NZ)]
 ROW = [(0, b, d) for b in range(NX) for d in range(2)][1:]
 
-ORDER = [[7, 6, 5, 4, 1, 2, 3], [6, 5, 4, 3, 7, 1, 2], [2, 3, 4, 5, 6, 7, 1], [5, 6, 7, 1, 2, 3, 4], [4, 5, 6, 7, 1, 2, 3], [3, 4, 5, 6, 7, 1, 2], [2, 3, 4, 5, 6, 7, 1], [1, 2, 3, 4, 5, 6, 7]]
+ORDER = [[1, 7, 6, 5, 4, 2, 3], [7, 6, 5, 4, 3, 1, 2], [2, 3, 4, 5, 6, 7, 1], [5, 6, 7, 1, 2, 3, 4], [4, 5, 6, 7, 1, 2, 3], [3, 4, 5, 6, 7, 1, 2], [2, 3, 4, 5, 6, 7, 1], [1, 2, 3, 4, 5, 6, 7]]
 
 
 def iota(shape, dim):

time: 38 us -> 38 us (level)
  no operation moved by 1% of the time
where the time goes in v5:
time: 38 us; the launch traced here: 37.6 us
  Pallas kernels  35.7 us (94%)
  local copies, waits for them, and re-layouts  1.89 us (5%)
    pallas_call x1, Pallas kernels, per_device(): pl.pallas_call(kernel, out_shape=jax.ShapeDtypeStruct((ROWS, ELEM), F32),...  35.7 us
    unnamed x1, local copies, waits for them, and re-layouts  1.89 us

profile of v5, /device:TPU:1, one launch (start us, length us, event | category | flops | bytes accessed | tf_op | source)
XLA Modules:
  0.0 37.6 jit_solution(13845198296124776884)
XLA Ops:
  0.0 35.7 %shard_map.109 = f32[1024,128]{1,0:T(8,128)} custom-call(f32[1024,128]{1,0:T(8,128)} %bitcast.10, f32[1024,128]{1,0:T(8,128)} %bitcast.11, f32[3,128]{1,0:T(4,128)} %vel_in.1, f32[192,64]{1,0:T(8,128)} %bitcast.12, f32[64,96]{1,0:T(8,128)} %lift_in.1, bf16[128,128]{1,0:T(8,128)(2,1)} %sto_in.1, s32[2,64]{1,0:T(2,128)} %bitcast.13, s32[6,128]{1,0:T(8,128)} %nbr_in.1, ...), custom_call_target="tpu_custom_call" | custom-call | tf_op jit(solution)/shard_map/pallas_call | solution.py:375
  35.7 1.9 %copy.13 = f32[16,64,128]{2,1,0:T(8,128)} copy(f32[16,64,128]{2,1,0:T(8,128)} %bitcast.9) | data formatting | bytes 1048576
